TPU v7x, 256 devices: a whole 4x4x8 slice. The times are simulated.
256 devices in a mesh: gx: 8 (over y, core), gy: 8 (over z_hi, x), af: 4 (over z_lo).
Axes of the slice: x: 4, y: 4, z: 8 (z_hi: 2, z_lo: 4; z = z_hi * 4 + z_lo), core: 2. Of those that a mesh axis runs over, the one named last changes fastest.
Arguments:
- volume: bfloat16 [32, 32, 128, 128], P('af', 'gx', 'gy'), may hold values from -6 to 6
- weight_one: bfloat16 [32, 32, 3, 3, 3], P('af'), may hold values from -0.21875 to 0.21875
- bias_one: float32 [32], P('af'), may hold values from -1 to 1
- weight_two: bfloat16 [32, 32, 3, 3, 3], P('af'), may hold values from -0.21875 to 0.21875
- cotangent: bfloat16 [32, 32, 128, 128], P('af', 'gx', 'gy'), may hold values from -6 to 6
Outputs:
- output: bfloat16 [32, 32, 128, 128], P('af', 'gx', 'gy')
- input_grad: bfloat16 [32, 32, 128, 128], P('af', 'gx', 'gy')
- grad_one: float32 [32, 32, 3, 3, 3], P('af')
- bias_grad: float32 [32], P('af')
- grad_two: float32 [32, 32, 3, 3, 3], P('af')
All inputs are finite; a program needn't handle non-finite values.
Results may differ from a plain program's by a relative error of at most 0.0065.
Values may be sent and summed in bfloat16 or wider, within the bound.
A program may use at most 64 MiB of HBM per device.

v0:
```python
import math
import jax
import jax.numpy as jnp
from jax import lax
from jax.sharding import PartitionSpec as P


def with_halo(cells, sides, width):
    for axis, dim in sides:
        count = lax.axis_size(axis)
        ends = count - 1
        head = lax.slice_in_dim(cells, 0, width, axis=dim)
        tail = lax.slice_in_dim(cells, cells.shape[dim] - width, cells.shape[dim], axis=dim)
        cells = jnp.concatenate(
            [
                lax.ppermute(tail, axis, [(i, (i + 1) % count) for i in range(ends)]),
                cells,
                lax.ppermute(head, axis, [((i + 1) % count, i) for i in range(ends)]),
            ],
            axis=dim,
        )
    return cells


def conv_valid(padded, weight):
    size_x = padded.shape[1] - 2
    size_y = padded.shape[2] - 2
    size_z = padded.shape[3] - 2
    total = jnp.zeros((weight.shape[0], size_x, size_y, size_z), jnp.float32)
    for off_x in range(3):
        for off_y in range(3):
            for off_z in range(3):
                window = padded[
                    :, off_x : off_x + size_x, off_y : off_y + size_y, off_z : off_z + size_z
                ]
                total = total + jnp.einsum(
                    "oi,ixyz->oxyz",
                    weight[:, :, off_x, off_y, off_z],
                    window,
                    preferred_element_type=jnp.float32,
                )
    return total


def kernel_grad(padded, cot_field):
    size_x = cot_field.shape[1]
    size_y = cot_field.shape[2]
    size_z = cot_field.shape[3]
    blocks = []
    for off_x in range(3):
        for off_y in range(3):
            for off_z in range(3):
                window = padded[
                    :, off_x : off_x + size_x, off_y : off_y + size_y, off_z : off_z + size_z
                ]
                blocks.append(
                    jnp.einsum(
                        "oxyz,ixyz->oi", cot_field, window, preferred_element_type=jnp.float32
                    )
                )
    stacked = jnp.stack(blocks, axis=-1)
    return stacked.reshape(cot_field.shape[0], padded.shape[0], 3, 3, 3)


def flipped(weight):
    return jnp.transpose(jnp.flip(weight, (2, 3, 4)), (1, 0, 2, 3, 4))


def depth_pad(values):
    return jnp.pad(values, ((0, 0), (0, 0), (0, 0), (1, 1)))


def full_padded(values):
    gathered = lax.all_gather(values, "af", axis=0, tiled=True)
    rimmed = with_halo(gathered, (("gx", 1), ("gy", 2)), 1)
    return depth_pad(rimmed)


def silu_grad(hidden_grad, pre_act):
    sigma_vals = jax.nn.sigmoid(pre_act)
    return (hidden_grad * sigma_vals * (1.0 + pre_act * (1.0 - sigma_vals))).astype(jnp.bfloat16)


def body(volume, weight_one, bias_one, weight_two, cotangent):
    own_rows = volume.shape[0]
    vol_pad = full_padded(volume)
    pre_act = conv_valid(vol_pad, weight_one) + bias_one[:, None, None, None]
    hidden = jax.nn.silu(pre_act).astype(jnp.bfloat16)
    hid_pad = full_padded(hidden)
    output = conv_valid(hid_pad, weight_two).astype(jnp.bfloat16)
    local_two = kernel_grad(hid_pad, cotangent)
    every_one, every_two = (
        lax.all_gather(weight_one, "af", axis=0, tiled=True),
        lax.all_gather(weight_two, "af", axis=0, tiled=True),
    )
    first_row = lax.axis_index("af") * own_rows

    def transposed(cot_field, every_w):
        padded = full_padded(cot_field)
        turned = lax.dynamic_slice_in_dim(flipped(every_w), first_row, own_rows, 0)
        return conv_valid(padded, turned)

    hidden_grad = transposed(cotangent, every_two)
    pre_grad = silu_grad(hidden_grad, pre_act)
    local_one = kernel_grad(vol_pad, pre_grad)
    local_bias = jnp.sum(pre_grad, axis=(1, 2, 3), dtype=jnp.float32)
    input_grad = transposed(pre_grad, every_one).astype(jnp.bfloat16)
    summed_one, summed_bias, summed_two = lax.psum((local_one, local_bias, local_two), ("gx", "gy"))
    cell_total = (
        volume.shape[1]
        * lax.axis_size("gx")
        * volume.shape[2]
        * lax.axis_size("gy")
        * volume.shape[3]
    )
    grad_scale = 1.0 / math.sqrt(cell_total)
    return (
        output,
        input_grad,
        summed_one * grad_scale,
        summed_bias * grad_scale,
        summed_two * grad_scale,
    )


def solution(mesh):
    return jax.shard_map(
        body,
        mesh=mesh,
        in_specs=(
            P("af", "gx", "gy", None),
            P("af", None, None, None, None),
            P("af"),
            P("af", None, None, None, None),
            P("af", "gx", "gy", None),
        ),
        out_specs=(
            P("af", "gx", "gy", None),
            P("af", "gx", "gy", None),
            P("af", None, None, None, None),
            P("af"),
            P("af", None, None, None, None),
        ),
        check_vma=False,
    )
```

profile of v0, /device:TPU:0, one launch (start us, length us, event | category | flops | bytes accessed | tf_op | source)
XLA Modules:
  0.0 645.6 jit_solution(11498958030644135914)
XLA Ops:
  1.7 14.6 %all_gather.18 = bf16[32,4,16,128]{3,0,2,1:T(8,128)(2,1)S(1)} all-gather(bf16[8,4,16,128]{3,0,2,1:T(8,128)(2,1)S(1)} %copy.43), channel_id=1, replica_groups=mesh['gx'=8,'gy'=8,'af'=4] {'af'}, dimensions={0}, use_global_device_ids=true | all-gather | bytes 655360 | tf_op jit(solution)/shard_map/all_gather | solution.py:74
  16.3 1.3 collective-permute-start
  17.6 1.3 collective-permute-start.1
  19.9 15.3 %all_gather.22 = bf16[32,4,16,128]{3,0,2,1:T(8,128)(2,1)S(1)} all-gather(bf16[8,4,16,128]{3,0,2,1:T(8,128)(2,1)S(1)} %copy.46), channel_id=1, replica_groups=mesh['gx'=8,'gy'=8,'af'=4] {'af'}, dimensions={0}, use_global_device_ids=true | all-gather | bytes 655360 | tf_op jit(solution)/shard_map/all_gather | solution.py:74
  35.2 2.1 collective-permute-start.8
  37.4 1.3 collective-permute-start.9
  38.9 13.0 %all_gather.21 = bf16[32,32,3,3,3]{1,0,4,3,2:T(8,128)(2,1)S(1)} all-gather(bf16[8,32,3,3,3]{1,0,4,3,2:T(8,128)(2,1)S(1)} %copy-done.48), channel_id=1, replica_groups=mesh['gx'=8,'gy'=8,'af'=4] {'af'}, dimensions={0}, use_global_device_ids=true | all-gather | bytes 69120 | tf_op jit(solution)/shard_map/all_gather | solution.py:94
  52.3 13.0 %all_gather.20 = bf16[32,32,3,3,3]{1,0,4,3,2:T(8,128)(2,1)S(1)} all-gather(bf16[8,32,3,3,3]{1,0,4,3,2:T(8,128)(2,1)S(1)} %copy-done.50), channel_id=1, replica_groups=mesh['gx'=8,'gy'=8,'af'=4] {'af'}, dimensions={0}, use_global_device_ids=true | all-gather | bytes 69120 | tf_op jit(solution)/shard_map/all_gather | solution.py:93
  66.0 3.4 collective-permute-start.2
  69.4 1.3 collective-permute-start.3
  71.2 4.5 collective-permute-start.10
  75.8 1.5 collective-permute-start.11
  92.0 15.4 %all_gather.23 = bf16[32,4,16,128]{3,0,2,1:T(8,128)(2,1)S(1)} all-gather(bf16[8,4,16,128]{3,0,2,1:T(8,128)(2,1)S(1)} %get-tuple-element.51), channel_id=1, replica_groups=mesh['gx'=8,'gy'=8,'af'=4] {'af'}, dimensions={0}, use_global_device_ids=true | all-gather | bytes 655360 | tf_op jit(solution)/shard_map/all_gather | solution.py:74
  107.4 14.4 %all_gather.19 = bf16[32,4,16,128]{3,0,2,1:T(8,128)(2,1)S(1)} all-gather(bf16[8,4,16,128]{3,0,2,1:T(8,128)(2,1)S(1)} %get-tuple-element.48), channel_id=1, replica_groups=mesh['gx'=8,'gy'=8,'af'=4] {'af'}, dimensions={0}, use_global_device_ids=true | all-gather | bytes 655360 | tf_op jit(solution)/shard_map/all_gather | solution.py:74
  122.7 1.3 collective-permute-start.4
  123.9 1.5 collective-permute-start.5
  132.2 8.9 %collective-permute-start.12 = (bf16[32,1,16,128]{3,0,2,1:T(8,128)(2,1)S(1)}, bf16[32,1,16,128]{3,0,2,1:T(8,128)(2,1)S(1)}, u32[]{:S(2)}, u32[]{:S(2)}) collective-permute-start(bf16[32,1,16,128]{3,0,2,1:T(8,128)(2,1)S(1)} %get-tuple-element.27), channel_id=1, source_target_pairs={{0,32},{32,64},{64,96},{96,128},{128,160},{160,192},{192,224},{1,3... | collective-permute-start | bytes 393224 | tf_op jit(solution)/shard_map/ppermute | solution.py:16
  141.1 1.3 collective-permute-start.13
  144.3 4.4 collective-permute-start.6
  148.7 1.3 collective-permute-start.7
  150.2 9.7 %collective-permute-start.14 = (bf16[32,6,1,128]{3,0,2,1:T(8,128)(2,1)S(1)}, bf16[32,6,1,128]{3,0,2,1:T(8,128)(2,1)S(1)}, u32[]{:S(2)}, u32[]{:S(2)}) collective-permute-start(bf16[32,6,1,128]{3,0,2,1:T(8,128)(2,1)S(1)} %get-tuple-element.18), channel_id=1, source_target_pairs={{0,4},{4,8},{8,12},{12,16},{16,20},{20,24},{24,28},{1,5},{5,9},{9,... | collective-permute-start | bytes 147464 | tf_op jit(solution)/shard_map/ppermute | solution.py:16
  160.0 1.3 collective-permute-start.15
  164.8 7.0 %collective-permute-done.15 = bf16[32,6,1,128]{3,0,2,1:T(8,128)(2,1)S(1)} collective-permute-done((bf16[32,6,1,128]{3,0,2,1:T(8,128)(2,1)S(1)}, bf16[32,6,1,128]{3,0,2,1:T(8,128)(2,1)S(1)}, u32[]{:S(2)}, u32[]{:S(2)}) %collective-permute-start.15) | collective-permute-done | bytes 49184 | tf_op jit(solution)/shard_map/ppermute | solution.py:18
  192.3 1.1 fusion.316
  196.1 1.1 fusion.328
  198.1 1.1 convolution_bitcast_fusion.11
  203.0 1.1 convolution_bitcast_fusion.9
  213.4 413.0 %all-reduce.4 = (f32[8,32,3,3,3]{1,0,4,3,2:T(8,128)}, f32[8]{0:T(128)S(1)}, f32[8,32,3,3,3]{1,0,4,3,2:T(8,128)}) all-reduce(f32[8,32,3,3,3]{1,0,4,3,2:T(8,128)} %bitcast.1393, f32[8]{0:T(128)S(1)} %get-tuple-element.50, f32[8,32,3,3,3]{1,0,4,3,2:T(8,128)} %bitcast.1394), channel_id=1, replica_groups=mesh['gx'=8,'gy'=8,'af'=4] {'gx','gy'}, use_global_device_ids=true, to_apply=%region_0.1 | all-reduce | flops 13832 | bytes 110656 | tf_op jit(solution)/shard_map/psum | solution.py:108
  627.0 1.4 fusion.187
  628.3 1.2 fusion.181
  634.5 1.1 fusion.108
  643.1 1.1 fusion.109
  (325 shorter events, 82.5 us)
Async XLA Ops:
  0.6 38.1 %copy-start.50 = (bf16[8,32,3,3,3]{1,0,4,3,2:T(8,128)(2,1)S(1)}, bf16[8,32,3,3,3]{1,0,4,3,2:T(8,128)(2,1)}, u32[]{:S(2)}) copy-start(bf16[8,32,3,3,3]{1,0,4,3,2:T(8,128)(2,1)} %param.6) | copy-start | bytes 41476
  1.7 37.2 %copy-start.48 = (bf16[8,32,3,3,3]{1,0,4,3,2:T(8,128)(2,1)S(1)}, bf16[8,32,3,3,3]{1,0,4,3,2:T(8,128)(2,1)}, u32[]{:S(2)}) copy-start(bf16[8,32,3,3,3]{1,0,4,3,2:T(8,128)(2,1)} %param.8) | copy-start | bytes 41476
  16.3 49.2 %collective-permute-start = (bf16[32,1,16,128]{3,0,2,1:T(8,128)(2,1)S(1)}, bf16[32,1,16,128]{3,0,2,1:T(8,128)(2,1)S(1)}, u32[]{:S(2)}, u32[]{:S(2)}) collective-permute-start(bf16[32,1,16,128]{3,0,2,1:T(8,128)(2,1)S(1)} %get-tuple-element.39), channel_id=1, source_target_pairs={{0,32},{32,64},{64,96},{96,128},{128,160},{160,192},{192,224},{1,3... | collective-permute-start | bytes 393224 | tf_op jit(solution)/shard_map/ppermute | solution.py:16
  17.6 48.3 %collective-permute-start.1 = (bf16[32,1,16,128]{3,0,2,1:T(8,128)(2,1)S(1)}, bf16[32,1,16,128]{3,0,2,1:T(8,128)(2,1)S(1)}, u32[]{:S(2)}, u32[]{:S(2)}) collective-permute-start(bf16[32,1,16,128]{3,0,2,1:T(8,128)(2,1)S(1)} %get-tuple-element.38), channel_id=1, source_target_pairs={{32,0},{64,32},{96,64},{128,96},{160,128},{192,160},{224,192},{33,... | collective-permute-start | bytes 393224 | tf_op jit(solution)/shard_map/ppermute | solution.py:18
  35.2 35.8 %collective-permute-start.8 = (bf16[32,1,16,128]{3,0,2,1:T(8,128)(2,1)S(1)}, bf16[32,1,16,128]{3,0,2,1:T(8,128)(2,1)S(1)}, u32[]{:S(2)}, u32[]{:S(2)}) collective-permute-start(bf16[32,1,16,128]{3,0,2,1:T(8,128)(2,1)S(1)} %get-tuple-element.29), channel_id=1, source_target_pairs={{0,32},{32,64},{64,96},{96,128},{128,160},{160,192},{192,224},{1,3... | collective-permute-start | bytes 393224 | tf_op jit(solution)/shard_map/ppermute | solution.py:16
  37.4 33.8 %collective-permute-start.9 = (bf16[32,1,16,128]{3,0,2,1:T(8,128)(2,1)S(1)}, bf16[32,1,16,128]{3,0,2,1:T(8,128)(2,1)S(1)}, u32[]{:S(2)}, u32[]{:S(2)}) collective-permute-start(bf16[32,1,16,128]{3,0,2,1:T(8,128)(2,1)S(1)} %get-tuple-element.28), channel_id=1, source_target_pairs={{32,0},{64,32},{96,64},{128,96},{160,128},{192,160},{224,192},{33,... | collective-permute-start | bytes 393224 | tf_op jit(solution)/shard_map/ppermute | solution.py:18
  65.5 121.7 %copy-start.47 = (bf16[8,32,3,3,3]{1,0,4,3,2:T(8,128)(2,1)}, bf16[8,32,3,3,3]{1,0,4,3,2:T(8,128)(2,1)S(1)}, u32[]{:S(2)}) copy-start(bf16[8,32,3,3,3]{1,0,4,3,2:T(8,128)(2,1)S(1)} %dynamic-slice_bitcast_fusion.1) | copy-start | bytes 41476
  66.0 11.6 %collective-permute-start.2 = (bf16[32,6,1,128]{3,0,2,1:T(8,128)(2,1)S(1)}, bf16[32,6,1,128]{3,0,2,1:T(8,128)(2,1)S(1)}, u32[]{:S(2)}, u32[]{:S(2)}) collective-permute-start(bf16[32,6,1,128]{3,0,2,1:T(8,128)(2,1)S(1)} %get-tuple-element.24), channel_id=1, source_target_pairs={{0,4},{4,8},{8,12},{12,16},{16,20},{20,24},{24,28},{1,5},{5,9},{9,... | collective-permute-start | bytes 147464 | tf_op jit(solution)/shard_map/ppermute | solution.py:16
  69.4 8.3 %collective-permute-start.3 = (bf16[32,6,1,128]{3,0,2,1:T(8,128)(2,1)S(1)}, bf16[32,6,1,128]{3,0,2,1:T(8,128)(2,1)S(1)}, u32[]{:S(2)}, u32[]{:S(2)}) collective-permute-start(bf16[32,6,1,128]{3,0,2,1:T(8,128)(2,1)S(1)} %get-tuple-element.25), channel_id=1, source_target_pairs={{4,0},{8,4},{12,8},{16,12},{20,16},{24,20},{28,24},{5,1},{9,5},{13... | collective-permute-start | bytes 147464 | tf_op jit(solution)/shard_map/ppermute | solution.py:18
  71.2 11.8 %collective-permute-start.10 = (bf16[32,6,1,128]{3,0,2,1:T(8,128)(2,1)S(1)}, bf16[32,6,1,128]{3,0,2,1:T(8,128)(2,1)S(1)}, u32[]{:S(2)}, u32[]{:S(2)}) collective-permute-start(bf16[32,6,1,128]{3,0,2,1:T(8,128)(2,1)S(1)} %get-tuple-element.20), channel_id=1, source_target_pairs={{0,4},{4,8},{8,12},{12,16},{16,20},{20,24},{24,28},{1,5},{5,9},{9,... | collective-permute-start | bytes 147464 | tf_op jit(solution)/shard_map/ppermute | solution.py:16
  75.8 7.3 %collective-permute-start.11 = (bf16[32,6,1,128]{3,0,2,1:T(8,128)(2,1)S(1)}, bf16[32,6,1,128]{3,0,2,1:T(8,128)(2,1)S(1)}, u32[]{:S(2)}, u32[]{:S(2)}) collective-permute-start(bf16[32,6,1,128]{3,0,2,1:T(8,128)(2,1)S(1)} %get-tuple-element.21), channel_id=1, source_target_pairs={{4,0},{8,4},{12,8},{16,12},{20,16},{24,20},{28,24},{5,1},{9,5},{13... | collective-permute-start | bytes 147464 | tf_op jit(solution)/shard_map/ppermute | solution.py:18
  122.7 21.2 %collective-permute-start.4 = (bf16[32,1,16,128]{3,0,2,1:T(8,128)(2,1)S(1)}, bf16[32,1,16,128]{3,0,2,1:T(8,128)(2,1)S(1)}, u32[]{:S(2)}, u32[]{:S(2)}) collective-permute-start(bf16[32,1,16,128]{3,0,2,1:T(8,128)(2,1)S(1)} %get-tuple-element.34), channel_id=1, source_target_pairs={{0,32},{32,64},{64,96},{96,128},{128,160},{160,192},{192,224},{1,3... | collective-permute-start | bytes 393224 | tf_op jit(solution)/shard_map/ppermute | solution.py:16
  123.9 20.3 %collective-permute-start.5 = (bf16[32,1,16,128]{3,0,2,1:T(8,128)(2,1)S(1)}, bf16[32,1,16,128]{3,0,2,1:T(8,128)(2,1)S(1)}, u32[]{:S(2)}, u32[]{:S(2)}) collective-permute-start(bf16[32,1,16,128]{3,0,2,1:T(8,128)(2,1)S(1)} %get-tuple-element.33), channel_id=1, source_target_pairs={{32,0},{64,32},{96,64},{128,96},{160,128},{192,160},{224,192},{33,... | collective-permute-start | bytes 393224 | tf_op jit(solution)/shard_map/ppermute | solution.py:18
  132.2 17.8 %collective-permute-start.12 = (bf16[32,1,16,128]{3,0,2,1:T(8,128)(2,1)S(1)}, bf16[32,1,16,128]{3,0,2,1:T(8,128)(2,1)S(1)}, u32[]{:S(2)}, u32[]{:S(2)}) collective-permute-start(bf16[32,1,16,128]{3,0,2,1:T(8,128)(2,1)S(1)} %get-tuple-element.27), channel_id=1, source_target_pairs={{0,32},{32,64},{64,96},{96,128},{128,160},{160,192},{192,224},{1,3... | collective-permute-start | bytes 393224 | tf_op jit(solution)/shard_map/ppermute | solution.py:16
  141.1 9.1 %collective-permute-start.13 = (bf16[32,1,16,128]{3,0,2,1:T(8,128)(2,1)S(1)}, bf16[32,1,16,128]{3,0,2,1:T(8,128)(2,1)S(1)}, u32[]{:S(2)}, u32[]{:S(2)}) collective-permute-start(bf16[32,1,16,128]{3,0,2,1:T(8,128)(2,1)S(1)} %get-tuple-element.26), channel_id=1, source_target_pairs={{32,0},{64,32},{96,64},{128,96},{160,128},{192,160},{224,192},{33,... | collective-permute-start | bytes 393224 | tf_op jit(solution)/shard_map/ppermute | solution.py:18
  143.8 6.3 copy-start.51
  144.3 67.9 %copy-start.3 = (bf16[32,6,16,128]{3,0,2,1:T(8,128)(2,1)}, bf16[32,6,16,128]{3,0,2,1:T(8,128)(2,1)S(1)}, u32[]{:S(2)}) copy-start(bf16[32,6,16,128]{3,0,2,1:T(8,128)(2,1)S(1)} %get-tuple-element.43) | copy-start | bytes 2359300
  144.3 43.9 %collective-permute-start.6 = (bf16[32,6,1,128]{3,0,2,1:T(8,128)(2,1)S(1)}, bf16[32,6,1,128]{3,0,2,1:T(8,128)(2,1)S(1)}, u32[]{:S(2)}, u32[]{:S(2)}) collective-permute-start(bf16[32,6,1,128]{3,0,2,1:T(8,128)(2,1)S(1)} %get-tuple-element.22), channel_id=1, source_target_pairs={{0,4},{4,8},{8,12},{12,16},{16,20},{20,24},{24,28},{1,5},{5,9},{9,... | collective-permute-start | bytes 147464 | tf_op jit(solution)/shard_map/ppermute | solution.py:16
  148.7 39.5 %collective-permute-start.7 = (bf16[32,6,1,128]{3,0,2,1:T(8,128)(2,1)S(1)}, bf16[32,6,1,128]{3,0,2,1:T(8,128)(2,1)S(1)}, u32[]{:S(2)}, u32[]{:S(2)}) collective-permute-start(bf16[32,6,1,128]{3,0,2,1:T(8,128)(2,1)S(1)} %get-tuple-element.23), channel_id=1, source_target_pairs={{4,0},{8,4},{12,8},{16,12},{20,16},{24,20},{28,24},{5,1},{9,5},{13... | collective-permute-start | bytes 147464 | tf_op jit(solution)/shard_map/ppermute | solution.py:18
  150.2 21.7 %copy-start = (bf16[32,6,16,128]{3,0,2,1:T(8,128)(2,1)}, bf16[32,6,16,128]{3,0,2,1:T(8,128)(2,1)S(1)}, u32[]{:S(2)}) copy-start(bf16[32,6,16,128]{3,0,2,1:T(8,128)(2,1)S(1)} %constant_dynamic-update-slice_fusion.17) | copy-start | bytes 2359300
  150.2 14.6 %collective-permute-start.14 = (bf16[32,6,1,128]{3,0,2,1:T(8,128)(2,1)S(1)}, bf16[32,6,1,128]{3,0,2,1:T(8,128)(2,1)S(1)}, u32[]{:S(2)}, u32[]{:S(2)}) collective-permute-start(bf16[32,6,1,128]{3,0,2,1:T(8,128)(2,1)S(1)} %get-tuple-element.18), channel_id=1, source_target_pairs={{0,4},{4,8},{8,12},{12,16},{16,20},{20,24},{24,28},{1,5},{5,9},{9,... | collective-permute-start | bytes 147464 | tf_op jit(solution)/shard_map/ppermute | solution.py:16
  160.0 11.9 %collective-permute-start.15 = (bf16[32,6,1,128]{3,0,2,1:T(8,128)(2,1)S(1)}, bf16[32,6,1,128]{3,0,2,1:T(8,128)(2,1)S(1)}, u32[]{:S(2)}, u32[]{:S(2)}) collective-permute-start(bf16[32,6,1,128]{3,0,2,1:T(8,128)(2,1)S(1)} %get-tuple-element.19), channel_id=1, source_target_pairs={{4,0},{8,4},{12,8},{16,12},{20,16},{24,20},{28,24},{5,1},{9,5},{13... | collective-permute-start | bytes 147464 | tf_op jit(solution)/shard_map/ppermute | solution.py:18
  164.8 9.9 %copy-start.43 = (bf16[32,6,1,128]{3,0,2,1:T(8,128)(2,1)}, bf16[32,6,1,128]{3,0,2,1:T(8,128)(2,1)S(1)}, u32[]{:S(2)}) copy-start(bf16[32,6,1,128]{3,0,2,1:T(8,128)(2,1)S(1)} %collective-permute-done.14) | copy-start | bytes 147460
  188.3 21.9 %copy-start.55 = (bf16[32,6,1,128]{3,0,2,1:T(8,128)(2,1)}, bf16[32,6,1,128]{3,0,2,1:T(8,128)(2,1)S(1)}, u32[]{:S(2)}) copy-start(bf16[32,6,1,128]{3,0,2,1:T(8,128)(2,1)S(1)} %collective-permute-done.6) | copy-start | bytes 147460
  188.3 23.9 %copy-start.57 = (bf16[32,6,1,128]{3,0,2,1:T(8,128)(2,1)}, bf16[32,6,1,128]{3,0,2,1:T(8,128)(2,1)S(1)}, u32[]{:S(2)}) copy-start(bf16[32,6,1,128]{3,0,2,1:T(8,128)(2,1)S(1)} %collective-permute-done.7) | copy-start | bytes 147460
  626.9 3.6 copy-start.36
  626.9 3.6 copy-start.37
  626.9 3.6 copy-start.38
  626.9 3.6 copy-start.39
  626.9 3.6 copy-start.40
  627.0 3.6 copy-start.41
  627.0 3.6 copy-start.42
  (44 other events, 114.9 us)
where the time goes:
time: 647 us; the launch traced here: 646 us
  blocking collectives  499 us (77%)
  matrix products  80.8 us (12%)
  starting transfers between devices  46.4 us (7%)
  waiting for transfers between devices  7.08 us (1%)
    psum x1, blocking collectives, body(): lax.psum((local_one, local_bias, local_two), ('gx', 'gy'))  413 us
    dot_general x108, matrix products, conv_valid(): jnp.einsum('oi,ixyz->oxyz', weight[:, :, off_x, off_y, off_z], window, pr...  65.3 us
    all_gather x4, blocking collectives, full_padded(): gathered = lax.all_gather(values, 'af', axis=0, tiled=True)  59.7 us
    ppermute x8, starting transfers between devices, with_halo(): lax.ppermute(tail, axis, [(i, (i + 1) % count) for i in range(ends)])  35.7 us
    dot_general x54, matrix products, kernel_grad(): jnp.einsum('oxyz,ixyz->oi', cot_field, window, preferred_element_type=jnp...  15.6 us
    all_gather x1, blocking collectives, body(): lax.all_gather(weight_one, 'af', axis=0, tiled=True)  13 us
    all_gather x1, blocking collectives, body(): lax.all_gather(weight_two, 'af', axis=0, tiled=True)  13 us
  transfers between devices with their start and end apart: 16, of which 1 were waited for; matrix products, arithmetic and copies ran while one was open for 6% of the time, Pallas kernels for 0%

commit v1 on v0

--- a/solution.py
+++ b/solution.py
@@ -105,7 +105,9 @@
     local_one = kernel_grad(vol_pad, pre_grad)
     local_bias = jnp.sum(pre_grad, axis=(1, 2, 3), dtype=jnp.float32)
     input_grad = transposed(pre_grad, every_one).astype(jnp.bfloat16)
-    summed_one, summed_bias, summed_two = lax.psum((local_one, local_bias, local_two), ("gx", "gy"))
+    summed_one, summed_bias, summed_two = lax.psum(
+        lax.psum((local_one, local_bias, local_two), "gx"), "gy"
+    )
     cell_total = (
         volume.shape[1]
         * lax.axis_size("gx")

time: 647 us -> 335 us (0.52)
  the two profiles are of different devices: /device:TPU:0 before, /device:TPU:4 now
where the time goes in v1:
time: 335 us; the launch traced here: 331 us
  blocking collectives  172 us (51%)
  matrix products  80.7 us (24%)
  starting transfers between devices  54.3 us (16%)
  waiting for transfers between devices  10.5 us (3%)
  local copies, waits for them, and re-layouts  5.88 us (2%)
  other arithmetic  4.83 us (1%)
    dot_general x108, matrix products, conv_valid(): jnp.einsum('oi,ixyz->oxyz', weight[:, :, off_x, off_y, off_z], window, pr...  65.2 us
    all_gather x4, blocking collectives, full_padded(): gathered = lax.all_gather(values, 'af', axis=0, tiled=True)  60.4 us
    psum x1, blocking collectives, body(): lax.psum(lax.psum((local_one, local_bias, local_two), 'gx'), 'gy')  58 us
    ppermute x8, starting transfers between devices, with_halo(): lax.ppermute(tail, axis, [(i, (i + 1) % count) for i in range(ends)])  39.9 us
    psum x1, blocking collectives, body(): lax.psum((local_one, local_bias, local_two), 'gx')  28 us
    dot_general x54, matrix products, kernel_grad(): jnp.einsum('oxyz,ixyz->oi', cot_field, window, preferred_element_type=jnp...  15.5 us
    ppermute x8, starting transfers between devices, with_halo(): lax.ppermute(head, axis, [((i + 1) % count, i) for i in range(ends)])  14.4 us
    all_gather x1, blocking collectives, body(): lax.all_gather(weight_one, 'af', axis=0, tiled=True)  13 us
  transfers between devices with their start and end apart: 16, of which 2 were waited for; matrix products, arithmetic and copies ran while one was open for 11% of the time, Pallas kernels for 0%

profile of v1, /device:TPU:4, one launch (start us, length us, event | category | flops | bytes accessed | tf_op | source)
XLA Modules:
  0.0 330.8 jit_solution(6309157259139881229)
XLA Ops:
  1.7 16.4 %all_gather.18 = bf16[32,4,16,128]{3,0,2,1:T(8,128)(2,1)S(1)} all-gather(bf16[8,4,16,128]{3,0,2,1:T(8,128)(2,1)S(1)} %copy.43), channel_id=1, replica_groups=mesh['gx'=8,'gy'=8,'af'=4] {'af'}, dimensions={0}, use_global_device_ids=true | all-gather | bytes 655360 | tf_op jit(solution)/shard_map/all_gather | solution.py:74
  18.1 1.3 collective-permute-start
  19.4 1.3 collective-permute-start.1
  21.7 15.3 %all_gather.22 = bf16[32,4,16,128]{3,0,2,1:T(8,128)(2,1)S(1)} all-gather(bf16[8,4,16,128]{3,0,2,1:T(8,128)(2,1)S(1)} %copy.46), channel_id=1, replica_groups=mesh['gx'=8,'gy'=8,'af'=4] {'af'}, dimensions={0}, use_global_device_ids=true | all-gather | bytes 655360 | tf_op jit(solution)/shard_map/all_gather | solution.py:74
  37.0 2.1 collective-permute-start.8
  39.1 1.3 collective-permute-start.9
  40.6 13.0 %all_gather.21 = bf16[32,32,3,3,3]{1,0,4,3,2:T(8,128)(2,1)S(1)} all-gather(bf16[8,32,3,3,3]{1,0,4,3,2:T(8,128)(2,1)S(1)} %copy-done.48), channel_id=1, replica_groups=mesh['gx'=8,'gy'=8,'af'=4] {'af'}, dimensions={0}, use_global_device_ids=true | all-gather | bytes 69120 | tf_op jit(solution)/shard_map/all_gather | solution.py:94
  54.0 13.0 %all_gather.20 = bf16[32,32,3,3,3]{1,0,4,3,2:T(8,128)(2,1)S(1)} all-gather(bf16[8,32,3,3,3]{1,0,4,3,2:T(8,128)(2,1)S(1)} %copy-done.50), channel_id=1, replica_groups=mesh['gx'=8,'gy'=8,'af'=4] {'af'}, dimensions={0}, use_global_device_ids=true | all-gather | bytes 69120 | tf_op jit(solution)/shard_map/all_gather | solution.py:93
  67.7 3.1 collective-permute-start.2
  70.9 2.7 collective-permute-start.3
  74.1 6.8 %collective-permute-start.10 = (bf16[32,6,1,128]{3,0,2,1:T(8,128)(2,1)S(1)}, bf16[32,6,1,128]{3,0,2,1:T(8,128)(2,1)S(1)}, u32[]{:S(2)}, u32[]{:S(2)}) collective-permute-start(bf16[32,6,1,128]{3,0,2,1:T(8,128)(2,1)S(1)} %get-tuple-element.23), channel_id=1, source_target_pairs={{0,4},{4,8},{8,12},{12,16},{16,20},{20,24},{24,28},{1,5},{5,9},{9,... | collective-permute-start | bytes 147464 | tf_op jit(solution)/shard_map/ppermute | solution.py:16
  81.0 2.2 collective-permute-start.11
  88.9 4.0 %collective-permute-done.11 = bf16[32,6,1,128]{3,0,2,1:T(8,128)(2,1)S(1)} collective-permute-done((bf16[32,6,1,128]{3,0,2,1:T(8,128)(2,1)S(1)}, bf16[32,6,1,128]{3,0,2,1:T(8,128)(2,1)S(1)}, u32[]{:S(2)}, u32[]{:S(2)}) %collective-permute-start.11) | collective-permute-done | bytes 49184 | tf_op jit(solution)/shard_map/ppermute | solution.py:18
  101.9 14.2 %all_gather.23 = bf16[32,4,16,128]{3,0,2,1:T(8,128)(2,1)S(1)} all-gather(bf16[8,4,16,128]{3,0,2,1:T(8,128)(2,1)S(1)} %get-tuple-element.54), channel_id=1, replica_groups=mesh['gx'=8,'gy'=8,'af'=4] {'af'}, dimensions={0}, use_global_device_ids=true | all-gather | bytes 655360 | tf_op jit(solution)/shard_map/all_gather | solution.py:74
  116.1 14.5 %all_gather.19 = bf16[32,4,16,128]{3,0,2,1:T(8,128)(2,1)S(1)} all-gather(bf16[8,4,16,128]{3,0,2,1:T(8,128)(2,1)S(1)} %get-tuple-element.51), channel_id=1, replica_groups=mesh['gx'=8,'gy'=8,'af'=4] {'af'}, dimensions={0}, use_global_device_ids=true | all-gather | bytes 655360 | tf_op jit(solution)/shard_map/all_gather | solution.py:74
  131.5 1.3 collective-permute-start.4
  132.8 1.8 collective-permute-start.5
  141.3 8.5 %collective-permute-start.12 = (bf16[32,1,16,128]{3,0,2,1:T(8,128)(2,1)S(1)}, bf16[32,1,16,128]{3,0,2,1:T(8,128)(2,1)S(1)}, u32[]{:S(2)}, u32[]{:S(2)}) collective-permute-start(bf16[32,1,16,128]{3,0,2,1:T(8,128)(2,1)S(1)} %get-tuple-element.30), channel_id=1, source_target_pairs={{0,32},{32,64},{64,96},{96,128},{128,160},{160,192},{192,224},{1,3... | collective-permute-start | bytes 393224 | tf_op jit(solution)/shard_map/ppermute | solution.py:16
  149.8 1.3 collective-permute-start.13
  153.0 9.9 %collective-permute-start.6 = (bf16[32,6,1,128]{3,0,2,1:T(8,128)(2,1)S(1)}, bf16[32,6,1,128]{3,0,2,1:T(8,128)(2,1)S(1)}, u32[]{:S(2)}, u32[]{:S(2)}) collective-permute-start(bf16[32,6,1,128]{3,0,2,1:T(8,128)(2,1)S(1)} %get-tuple-element.25), channel_id=1, source_target_pairs={{0,4},{4,8},{8,12},{12,16},{16,20},{20,24},{24,28},{1,5},{5,9},{9,... | collective-permute-start | bytes 147464 | tf_op jit(solution)/shard_map/ppermute | solution.py:16
  162.9 1.9 collective-permute-start.7
  165.0 6.9 %collective-permute-start.14 = (bf16[32,6,1,128]{3,0,2,1:T(8,128)(2,1)S(1)}, bf16[32,6,1,128]{3,0,2,1:T(8,128)(2,1)S(1)}, u32[]{:S(2)}, u32[]{:S(2)}) collective-permute-start(bf16[32,6,1,128]{3,0,2,1:T(8,128)(2,1)S(1)} %get-tuple-element.21), channel_id=1, source_target_pairs={{0,4},{4,8},{8,12},{12,16},{16,20},{20,24},{24,28},{1,5},{5,9},{9,... | collective-permute-start | bytes 147464 | tf_op jit(solution)/shard_map/ppermute | solution.py:16
  171.9 1.9 collective-permute-start.15
  177.5 6.5 %collective-permute-done.15 = bf16[32,6,1,128]{3,0,2,1:T(8,128)(2,1)S(1)} collective-permute-done((bf16[32,6,1,128]{3,0,2,1:T(8,128)(2,1)S(1)}, bf16[32,6,1,128]{3,0,2,1:T(8,128)(2,1)S(1)}, u32[]{:S(2)}, u32[]{:S(2)}) %collective-permute-start.15) | collective-permute-done | bytes 49184 | tf_op jit(solution)/shard_map/ppermute | solution.py:18
  208.1 1.1 fusion.328
  215.0 1.1 convolution_bitcast_fusion.9
  225.4 28.0 %all-reduce.5 = (f32[8,32,3,3,3]{1,0,4,3,2:T(8,128)}, f32[8]{0:T(128)S(1)}, f32[8,32,3,3,3]{1,0,4,3,2:T(8,128)}) all-reduce(f32[8,32,3,3,3]{1,0,4,3,2:T(8,128)} %bitcast.1393, f32[8]{0:T(128)S(1)} %get-tuple-element.53, f32[8,32,3,3,3]{1,0,4,3,2:T(8,128)} %bitcast.1394), channel_id=1, replica_groups=mesh['gx'=8,'gy'=8,'af'=4] {'gx'}, use_global_device_ids=true, to_apply=%region_0.1 | all-reduce | flops 13832 | bytes 110656 | tf_op jit(solution)/shard_map/psum | solution.py:109
  253.4 58.0 %all-reduce.4 = (f32[8,32,3,3,3]{1,0,4,3,2:T(8,128)}, f32[8]{0:T(128)S(1)}, f32[8,32,3,3,3]{1,0,4,3,2:T(8,128)}) all-reduce(f32[8,32,3,3,3]{1,0,4,3,2:T(8,128)} %get-tuple-element.18, f32[8]{0:T(128)S(1)} %get-tuple-element.19, f32[8,32,3,3,3]{1,0,4,3,2:T(8,128)} %get-tuple-element.20), channel_id=1, replica_groups=mesh['gx'=8,'gy'=8,'af'=4] {'gy'}, use_global_device_ids=true, to_apply=%region_1.2 | all-reduce | flops 13832 | bytes 110656 | tf_op jit(solution)/shard_map/psum | solution.py:108
  312.0 1.4 fusion.187
  313.3 1.2 fusion.181
  319.5 1.1 fusion.108
  328.1 1.1 fusion.109
  (326 shorter events, 84.6 us)
Async XLA Ops:
  0.6 39.8 %copy-start.50 = (bf16[8,32,3,3,3]{1,0,4,3,2:T(8,128)(2,1)S(1)}, bf16[8,32,3,3,3]{1,0,4,3,2:T(8,128)(2,1)}, u32[]{:S(2)}) copy-start(bf16[8,32,3,3,3]{1,0,4,3,2:T(8,128)(2,1)} %param.6) | copy-start | bytes 41476
  1.7 39.0 %copy-start.48 = (bf16[8,32,3,3,3]{1,0,4,3,2:T(8,128)(2,1)S(1)}, bf16[8,32,3,3,3]{1,0,4,3,2:T(8,128)(2,1)}, u32[]{:S(2)}) copy-start(bf16[8,32,3,3,3]{1,0,4,3,2:T(8,128)(2,1)} %param.8) | copy-start | bytes 41476
  18.1 49.2 %collective-permute-start = (bf16[32,1,16,128]{3,0,2,1:T(8,128)(2,1)S(1)}, bf16[32,1,16,128]{3,0,2,1:T(8,128)(2,1)S(1)}, u32[]{:S(2)}, u32[]{:S(2)}) collective-permute-start(bf16[32,1,16,128]{3,0,2,1:T(8,128)(2,1)S(1)} %get-tuple-element.42), channel_id=1, source_target_pairs={{0,32},{32,64},{64,96},{96,128},{128,160},{160,192},{192,224},{1,3... | collective-permute-start | bytes 393224 | tf_op jit(solution)/shard_map/ppermute | solution.py:16
  19.4 48.3 %collective-permute-start.1 = (bf16[32,1,16,128]{3,0,2,1:T(8,128)(2,1)S(1)}, bf16[32,1,16,128]{3,0,2,1:T(8,128)(2,1)S(1)}, u32[]{:S(2)}, u32[]{:S(2)}) collective-permute-start(bf16[32,1,16,128]{3,0,2,1:T(8,128)(2,1)S(1)} %get-tuple-element.41), channel_id=1, source_target_pairs={{32,0},{64,32},{96,64},{128,96},{160,128},{192,160},{224,192},{33,... | collective-permute-start | bytes 393224 | tf_op jit(solution)/shard_map/ppermute | solution.py:18
  37.0 37.0 %collective-permute-start.8 = (bf16[32,1,16,128]{3,0,2,1:T(8,128)(2,1)S(1)}, bf16[32,1,16,128]{3,0,2,1:T(8,128)(2,1)S(1)}, u32[]{:S(2)}, u32[]{:S(2)}) collective-permute-start(bf16[32,1,16,128]{3,0,2,1:T(8,128)(2,1)S(1)} %get-tuple-element.32), channel_id=1, source_target_pairs={{0,32},{32,64},{64,96},{96,128},{128,160},{160,192},{192,224},{1,3... | collective-permute-start | bytes 393224 | tf_op jit(solution)/shard_map/ppermute | solution.py:16
  39.1 34.9 %collective-permute-start.9 = (bf16[32,1,16,128]{3,0,2,1:T(8,128)(2,1)S(1)}, bf16[32,1,16,128]{3,0,2,1:T(8,128)(2,1)S(1)}, u32[]{:S(2)}, u32[]{:S(2)}) collective-permute-start(bf16[32,1,16,128]{3,0,2,1:T(8,128)(2,1)S(1)} %get-tuple-element.31), channel_id=1, source_target_pairs={{32,0},{64,32},{96,64},{128,96},{160,128},{192,160},{224,192},{33,... | collective-permute-start | bytes 393224 | tf_op jit(solution)/shard_map/ppermute | solution.py:18
  67.3 132.0 %copy-start.47 = (bf16[8,32,3,3,3]{1,0,4,3,2:T(8,128)(2,1)}, bf16[8,32,3,3,3]{1,0,4,3,2:T(8,128)(2,1)S(1)}, u32[]{:S(2)}) copy-start(bf16[8,32,3,3,3]{1,0,4,3,2:T(8,128)(2,1)S(1)} %dynamic-slice_bitcast_fusion.1) | copy-start | bytes 41476
  67.7 15.8 %collective-permute-start.2 = (bf16[32,6,1,128]{3,0,2,1:T(8,128)(2,1)S(1)}, bf16[32,6,1,128]{3,0,2,1:T(8,128)(2,1)S(1)}, u32[]{:S(2)}, u32[]{:S(2)}) collective-permute-start(bf16[32,6,1,128]{3,0,2,1:T(8,128)(2,1)S(1)} %get-tuple-element.27), channel_id=1, source_target_pairs={{0,4},{4,8},{8,12},{12,16},{16,20},{20,24},{24,28},{1,5},{5,9},{9,... | collective-permute-start | bytes 147464 | tf_op jit(solution)/shard_map/ppermute | solution.py:16
  70.9 12.7 %collective-permute-start.3 = (bf16[32,6,1,128]{3,0,2,1:T(8,128)(2,1)S(1)}, bf16[32,6,1,128]{3,0,2,1:T(8,128)(2,1)S(1)}, u32[]{:S(2)}, u32[]{:S(2)}) collective-permute-start(bf16[32,6,1,128]{3,0,2,1:T(8,128)(2,1)S(1)} %get-tuple-element.28), channel_id=1, source_target_pairs={{4,0},{8,4},{12,8},{16,12},{20,16},{24,20},{28,24},{5,1},{9,5},{13... | collective-permute-start | bytes 147464 | tf_op jit(solution)/shard_map/ppermute | solution.py:18
  74.1 14.8 %collective-permute-start.10 = (bf16[32,6,1,128]{3,0,2,1:T(8,128)(2,1)S(1)}, bf16[32,6,1,128]{3,0,2,1:T(8,128)(2,1)S(1)}, u32[]{:S(2)}, u32[]{:S(2)}) collective-permute-start(bf16[32,6,1,128]{3,0,2,1:T(8,128)(2,1)S(1)} %get-tuple-element.23), channel_id=1, source_target_pairs={{0,4},{4,8},{8,12},{12,16},{16,20},{20,24},{24,28},{1,5},{5,9},{9,... | collective-permute-start | bytes 147464 | tf_op jit(solution)/shard_map/ppermute | solution.py:16
  81.0 12.0 %collective-permute-start.11 = (bf16[32,6,1,128]{3,0,2,1:T(8,128)(2,1)S(1)}, bf16[32,6,1,128]{3,0,2,1:T(8,128)(2,1)S(1)}, u32[]{:S(2)}, u32[]{:S(2)}) collective-permute-start(bf16[32,6,1,128]{3,0,2,1:T(8,128)(2,1)S(1)} %get-tuple-element.24), channel_id=1, source_target_pairs={{4,0},{8,4},{12,8},{16,12},{20,16},{24,20},{28,24},{5,1},{9,5},{13... | collective-permute-start | bytes 147464 | tf_op jit(solution)/shard_map/ppermute | solution.py:18
  131.5 21.0 %collective-permute-start.4 = (bf16[32,1,16,128]{3,0,2,1:T(8,128)(2,1)S(1)}, bf16[32,1,16,128]{3,0,2,1:T(8,128)(2,1)S(1)}, u32[]{:S(2)}, u32[]{:S(2)}) collective-permute-start(bf16[32,1,16,128]{3,0,2,1:T(8,128)(2,1)S(1)} %get-tuple-element.37), channel_id=1, source_target_pairs={{0,32},{32,64},{64,96},{96,128},{128,160},{160,192},{192,224},{1,3... | collective-permute-start | bytes 393224 | tf_op jit(solution)/shard_map/ppermute | solution.py:16
  132.8 20.1 %collective-permute-start.5 = (bf16[32,1,16,128]{3,0,2,1:T(8,128)(2,1)S(1)}, bf16[32,1,16,128]{3,0,2,1:T(8,128)(2,1)S(1)}, u32[]{:S(2)}, u32[]{:S(2)}) collective-permute-start(bf16[32,1,16,128]{3,0,2,1:T(8,128)(2,1)S(1)} %get-tuple-element.36), channel_id=1, source_target_pairs={{32,0},{64,32},{96,64},{128,96},{160,128},{192,160},{224,192},{33,... | collective-permute-start | bytes 393224 | tf_op jit(solution)/shard_map/ppermute | solution.py:18
  141.3 23.5 %collective-permute-start.12 = (bf16[32,1,16,128]{3,0,2,1:T(8,128)(2,1)S(1)}, bf16[32,1,16,128]{3,0,2,1:T(8,128)(2,1)S(1)}, u32[]{:S(2)}, u32[]{:S(2)}) collective-permute-start(bf16[32,1,16,128]{3,0,2,1:T(8,128)(2,1)S(1)} %get-tuple-element.30), channel_id=1, source_target_pairs={{0,32},{32,64},{64,96},{96,128},{128,160},{160,192},{192,224},{1,3... | collective-permute-start | bytes 393224 | tf_op jit(solution)/shard_map/ppermute | solution.py:16
  149.8 15.1 %collective-permute-start.13 = (bf16[32,1,16,128]{3,0,2,1:T(8,128)(2,1)S(1)}, bf16[32,1,16,128]{3,0,2,1:T(8,128)(2,1)S(1)}, u32[]{:S(2)}, u32[]{:S(2)}) collective-permute-start(bf16[32,1,16,128]{3,0,2,1:T(8,128)(2,1)S(1)} %get-tuple-element.29), channel_id=1, source_target_pairs={{32,0},{64,32},{96,64},{128,96},{160,128},{192,160},{224,192},{33,... | collective-permute-start | bytes 393224 | tf_op jit(solution)/shard_map/ppermute | solution.py:18
  152.5 12.4 %copy-start.51 = (f32[8,32,27]{1,0,2:T(8,128)}, f32[8,32,27]{1,0,2:T(8,128)S(1)}, u32[]{:S(2)}) copy-start(f32[8,32,27]{1,0,2:T(8,128)S(1)} %fusion.138) | copy-start | bytes 82948
  153.0 71.1 %copy-start.3 = (bf16[32,6,16,128]{3,0,2,1:T(8,128)(2,1)}, bf16[32,6,16,128]{3,0,2,1:T(8,128)(2,1)S(1)}, u32[]{:S(2)}) copy-start(bf16[32,6,16,128]{3,0,2,1:T(8,128)(2,1)S(1)} %get-tuple-element.46) | copy-start | bytes 2359300
  153.0 47.3 %collective-permute-start.6 = (bf16[32,6,1,128]{3,0,2,1:T(8,128)(2,1)S(1)}, bf16[32,6,1,128]{3,0,2,1:T(8,128)(2,1)S(1)}, u32[]{:S(2)}, u32[]{:S(2)}) collective-permute-start(bf16[32,6,1,128]{3,0,2,1:T(8,128)(2,1)S(1)} %get-tuple-element.25), channel_id=1, source_target_pairs={{0,4},{4,8},{8,12},{12,16},{16,20},{20,24},{24,28},{1,5},{5,9},{9,... | collective-permute-start | bytes 147464 | tf_op jit(solution)/shard_map/ppermute | solution.py:16
  162.9 37.4 %collective-permute-start.7 = (bf16[32,6,1,128]{3,0,2,1:T(8,128)(2,1)S(1)}, bf16[32,6,1,128]{3,0,2,1:T(8,128)(2,1)S(1)}, u32[]{:S(2)}, u32[]{:S(2)}) collective-permute-start(bf16[32,6,1,128]{3,0,2,1:T(8,128)(2,1)S(1)} %get-tuple-element.26), channel_id=1, source_target_pairs={{4,0},{8,4},{12,8},{16,12},{20,16},{24,20},{28,24},{5,1},{9,5},{13... | collective-permute-start | bytes 147464 | tf_op jit(solution)/shard_map/ppermute | solution.py:18
  165.0 19.0 %copy-start = (bf16[32,6,16,128]{3,0,2,1:T(8,128)(2,1)}, bf16[32,6,16,128]{3,0,2,1:T(8,128)(2,1)S(1)}, u32[]{:S(2)}) copy-start(bf16[32,6,16,128]{3,0,2,1:T(8,128)(2,1)S(1)} %constant_dynamic-update-slice_fusion.17) | copy-start | bytes 2359300
  165.0 12.5 %collective-permute-start.14 = (bf16[32,6,1,128]{3,0,2,1:T(8,128)(2,1)S(1)}, bf16[32,6,1,128]{3,0,2,1:T(8,128)(2,1)S(1)}, u32[]{:S(2)}, u32[]{:S(2)}) collective-permute-start(bf16[32,6,1,128]{3,0,2,1:T(8,128)(2,1)S(1)} %get-tuple-element.21), channel_id=1, source_target_pairs={{0,4},{4,8},{8,12},{12,16},{16,20},{20,24},{24,28},{1,5},{5,9},{9,... | collective-permute-start | bytes 147464 | tf_op jit(solution)/shard_map/ppermute | solution.py:16
  171.9 12.0 %collective-permute-start.15 = (bf16[32,6,1,128]{3,0,2,1:T(8,128)(2,1)S(1)}, bf16[32,6,1,128]{3,0,2,1:T(8,128)(2,1)S(1)}, u32[]{:S(2)}, u32[]{:S(2)}) collective-permute-start(bf16[32,6,1,128]{3,0,2,1:T(8,128)(2,1)S(1)} %get-tuple-element.22), channel_id=1, source_target_pairs={{4,0},{8,4},{12,8},{16,12},{20,16},{24,20},{28,24},{5,1},{9,5},{13... | collective-permute-start | bytes 147464 | tf_op jit(solution)/shard_map/ppermute | solution.py:18
  177.5 9.3 %copy-start.43 = (bf16[32,6,1,128]{3,0,2,1:T(8,128)(2,1)}, bf16[32,6,1,128]{3,0,2,1:T(8,128)(2,1)S(1)}, u32[]{:S(2)}) copy-start(bf16[32,6,1,128]{3,0,2,1:T(8,128)(2,1)S(1)} %collective-permute-done.14) | copy-start | bytes 147460
  200.3 21.9 %copy-start.55 = (bf16[32,6,1,128]{3,0,2,1:T(8,128)(2,1)}, bf16[32,6,1,128]{3,0,2,1:T(8,128)(2,1)S(1)}, u32[]{:S(2)}) copy-start(bf16[32,6,1,128]{3,0,2,1:T(8,128)(2,1)S(1)} %collective-permute-done.6) | copy-start | bytes 147460
  200.3 23.8 %copy-start.57 = (bf16[32,6,1,128]{3,0,2,1:T(8,128)(2,1)}, bf16[32,6,1,128]{3,0,2,1:T(8,128)(2,1)S(1)}, u32[]{:S(2)}) copy-start(bf16[32,6,1,128]{3,0,2,1:T(8,128)(2,1)S(1)} %collective-permute-done.7) | copy-start | bytes 147460
  311.9 3.6 %copy-start.36 = (f32[8,4,16,128]{3,0,2,1:T(8,128)S(1)}, f32[8,4,16,128]{3,0,2,1:T(8,128)}, u32[]{:S(2)}) copy-start(f32[8,4,16,128]{3,0,2,1:T(8,128)} %fusion.228) | copy-start | bytes 786436
  311.9 3.6 %copy-start.37 = (f32[8,4,16,128]{3,0,2,1:T(8,128)S(1)}, f32[8,4,16,128]{3,0,2,1:T(8,128)}, u32[]{:S(2)}) copy-start(f32[8,4,16,128]{3,0,2,1:T(8,128)} %fusion.230) | copy-start | bytes 786436
  311.9 3.6 %copy-start.38 = (f32[8,4,16,128]{3,0,2,1:T(8,128)S(1)}, f32[8,4,16,128]{3,0,2,1:T(8,128)}, u32[]{:S(2)}) copy-start(f32[8,4,16,128]{3,0,2,1:T(8,128)} %fusion.232) | copy-start | bytes 786436
  311.9 3.6 %copy-start.39 = (f32[8,4,16,128]{3,0,2,1:T(8,128)S(1)}, f32[8,4,16,128]{3,0,2,1:T(8,128)}, u32[]{:S(2)}) copy-start(f32[8,4,16,128]{3,0,2,1:T(8,128)} %fusion.234) | copy-start | bytes 786436
  312.0 3.6 %copy-start.40 = (f32[8,4,16,128]{3,0,2,1:T(8,128)S(1)}, f32[8,4,16,128]{3,0,2,1:T(8,128)}, u32[]{:S(2)}) copy-start(f32[8,4,16,128]{3,0,2,1:T(8,128)} %fusion.236) | copy-start | bytes 786436
  312.0 3.6 %copy-start.41 = (f32[8,4,16,128]{3,0,2,1:T(8,128)S(1)}, f32[8,4,16,128]{3,0,2,1:T(8,128)}, u32[]{:S(2)}) copy-start(f32[8,4,16,128]{3,0,2,1:T(8,128)} %fusion.240) | copy-start | bytes 786436
  312.0 3.6 %copy-start.42 = (f32[8,4,16,128]{3,0,2,1:T(8,128)S(1)}, f32[8,4,16,128]{3,0,2,1:T(8,128)}, u32[]{:S(2)}) copy-start(f32[8,4,16,128]{3,0,2,1:T(8,128)} %fusion.242) | copy-start | bytes 786436
  (44 other events, 115.0 us)
